TPU v7x, 32 devices: a whole 2x2x4 slice. The times are simulated.
32 devices in a mesh: gx: 16 (over z, x, core), gy: 2 (over y).
Axes of the slice: x: 2, y: 2, z: 4, core: 2. Of those that a mesh axis runs over, the one named last changes fastest.
Arguments:
- potential: float32 [3, 1, 4096, 256], P(None, None, 'gx', 'gy'), may hold values from -8 to 8
- labels: int32 [1, 4096, 256], P(None, 'gx', 'gy'), may hold values from 0 to 7
- principal: float32 [2, 8], replicated, may hold values from 0.5 to 16
- off_diagonal: float32 [3, 8], replicated, may hold values from -0.4 to 0.4
Outputs:
- updated: float32 [3, 1, 4096, 256], P(None, None, 'gx', 'gy')
All inputs are finite; a program needn't handle non-finite values.
Results may differ from a plain program's by a relative error of at most 0.0017.
Values sent between devices are 32-bit elements; how exact they have to be, the bound alone decides.
A program may use at most 64 MiB of HBM per device.

v0:
```python
import jax
import jax.numpy as jnp
from jax import lax
from jax.sharding import PartitionSpec as P


def shifted_2(shard, axis, by):
    size = lax.axis_size(axis)
    return lax.ppermute(shard, axis, [(i, (i + by) % size) for i in range(size)])


def padded_2(cells, sides, width):
    for axis, dim in sides:
        count = lax.axis_size(axis)
        head = lax.slice_in_dim(cells, 0, width, axis=dim)
        tail = lax.slice_in_dim(cells, cells.shape[dim] - width, cells.shape[dim], axis=dim)
        cells = jnp.concatenate(
            [
                lax.ppermute(tail, axis, [(i, (i + 1) % count) for i in range(count)]),
                cells,
                lax.ppermute(head, axis, [((i + 1) % count, i) for i in range(count)]),
            ],
            axis=dim,
        )
    return cells


def harmonic(first, second):
    return 2.0 * first * second / (first + second)


def neighbour(values, offset, axis_dim, filler):
    extent = values.shape[axis_dim]
    dims_pad = list(values.shape)
    dims_pad[axis_dim] = abs(offset)
    padding = jnp.full(tuple(dims_pad), filler, values.dtype)
    if offset > 0:
        retained = lax.slice_in_dim(values, 0, extent - offset, axis=axis_dim)
        return jnp.concatenate([padding, retained], axis_dim)
    retained = lax.slice_in_dim(values, -offset, extent, axis=axis_dim)
    return jnp.concatenate([retained, padding], axis_dim)


def shifted(values, offset, axis_dim, wrap, filler):
    if wrap:
        return jnp.roll(values, offset, axis_dim)
    return neighbour(values, offset, axis_dim, filler)


def cyclic_reduce(sub_diag, main_diag, super_diag, forcing, axis_dim, wrap):
    extent = sub_diag.shape[axis_dim]
    stride = 1
    while stride < extent:
        low_before = shifted(sub_diag, stride, axis_dim, wrap, 0.0)
        main_before = shifted(main_diag, stride, axis_dim, wrap, 1.0)
        high_before = shifted(super_diag, stride, axis_dim, wrap, 0.0)
        rest_before = shifted(forcing, stride, axis_dim + 1, wrap, 0.0)
        low_after = shifted(sub_diag, -stride, axis_dim, wrap, 0.0)
        main_after = shifted(main_diag, -stride, axis_dim, wrap, 1.0)
        high_after = shifted(super_diag, -stride, axis_dim, wrap, 0.0)
        rest_after = shifted(forcing, -stride, axis_dim + 1, wrap, 0.0)
        factor_low = -sub_diag / main_before
        factor_high = -super_diag / main_after
        forcing = forcing + factor_low[None] * rest_before + factor_high[None] * rest_after
        main_diag = main_diag + factor_low * high_before + factor_high * low_after
        sub_diag = factor_low * low_before
        super_diag = factor_high * high_after
        stride = stride * 2
    return forcing / (sub_diag + main_diag + super_diag)[None]


def reduced_rows(tail_row, next_head, low_last, main_last, high_last, force_last):
    reduced_low = -low_last * tail_row[3]
    reduced_main = main_last - low_last * tail_row[4] - high_last * next_head[3]
    reduced_high = -high_last * next_head[4]
    reduced_force = force_last - low_last[None] * tail_row[:3] - high_last[None] * next_head[:3]
    return jnp.concatenate(
        [reduced_low[None], reduced_main[None], reduced_high[None], reduced_force], 0
    )


def spike_solve(sub_diag, main_diag, super_diag, forcing, axis_dim, interface):
    length = sub_diag.shape[axis_dim]
    position = lax.broadcasted_iota(jnp.int32, sub_diag.shape, axis_dim)
    is_last = position == length - 1
    low_inner = jnp.where((position == 0) | is_last, 0.0, sub_diag)
    high_inner = jnp.where((position == length - 2) | is_last, 0.0, super_diag)
    main_inner = jnp.where(is_last, 1.0, main_diag)
    left_spike = jnp.where(position == 0, sub_diag, 0.0)
    right_spike = jnp.where(position == length - 2, super_diag, 0.0)
    stacked = jnp.concatenate(
        [jnp.where(is_last[None], 0.0, forcing), left_spike[None], right_spike[None]], 0
    )
    solved = cyclic_reduce(low_inner, main_inner, high_inner, stacked, axis_dim, False)
    head_row = lax.slice_in_dim(solved, 0, 1, axis=axis_dim + 1)
    tail_row = lax.slice_in_dim(solved, length - 2, length - 1, axis=axis_dim + 1)
    low_last = lax.slice_in_dim(sub_diag, length - 1, length, axis=axis_dim)
    main_last = lax.slice_in_dim(main_diag, length - 1, length, axis=axis_dim)
    high_last = lax.slice_in_dim(super_diag, length - 1, length, axis=axis_dim)
    force_last = lax.slice_in_dim(forcing, length - 1, length, axis=axis_dim + 1)
    own_value, prev_value = interface(
        head_row, tail_row, low_last, main_last, high_last, force_last
    )
    inner_values = solved[:3] - solved[3][None] * prev_value - solved[4][None] * own_value
    return jnp.where(is_last[None], own_value, inner_values)


def pick_values(solution, members, my_index, axis_dim):
    own_value = lax.dynamic_slice_in_dim(solution, my_index, 1, axis_dim)
    prev_value = lax.dynamic_slice_in_dim(solution, (my_index + members - 1) % members, 1, axis_dim)
    return (own_value, prev_value)


def interface_x(head_row, tail_row, low_last, main_last, high_last, force_last):
    members = lax.axis_size("gx")
    my_index = lax.axis_index("gx")
    next_head = shifted_2(head_row, "gx", -1)
    rows_here = reduced_rows(tail_row, next_head, low_last, main_last, high_last, force_last)
    gathered = lax.all_gather(rows_here, "gx", axis=2, tiled=True)
    solution = cyclic_reduce(gathered[0], gathered[1], gathered[2], gathered[3:], 1, True)
    return pick_values(solution, members, my_index, 2)


def interface_y(head_row, tail_row, low_last, main_last, high_last, force_last):
    members = lax.axis_size("gy")
    next_head = shifted_2(head_row, "gy", -1)
    rows_here = reduced_rows(tail_row, next_head, low_last, main_last, high_last, force_last)
    gathered = lax.all_gather(rows_here, "gy", axis=3, tiled=True)
    solution = cyclic_reduce(gathered[0], gathered[1], gathered[2], gathered[3:], 2, True)
    return pick_values(solution, members, lax.axis_index("gy"), 3)


def lookup_phase(components, label_block):
    cell_tensor = jnp.zeros((5,) + label_block.shape, jnp.float32)
    for phase_id in range(components.shape[1]):
        cell_tensor = jnp.where(
            (label_block == phase_id)[None],
            components[:, phase_id][:, None, None, None],
            cell_tensor,
        )
    return cell_tensor


def local(potential, labels, principal, off_diagonal):
    components = jnp.concatenate([principal, off_diagonal], 0)
    cell_tensor = lookup_phase(components, labels)
    padded = padded_2(cell_tensor, (("gx", 2), ("gy", 3)), 1)
    damping = 2.0 / (potential.shape[3] * potential.shape[3])
    along_xdir = padded[:, :, :, 1:-1]
    cond_xx = along_xdir[0]
    face_east = harmonic(cond_xx[:, 1:-1], cond_xx[:, 2:])
    face_west = harmonic(cond_xx[:, :-2], cond_xx[:, 1:-1])
    source_x = jnp.stack(
        [
            face_east - face_west,
            0.5 * (along_xdir[2][:, 2:] - along_xdir[2][:, :-2]),
            0.5 * (along_xdir[3][:, 2:] - along_xdir[3][:, :-2]),
        ]
    )
    half_step = spike_solve(
        -face_west,
        damping + face_west + face_east,
        -face_east,
        damping * potential + source_x,
        1,
        interface_x,
    )
    along_ydir = padded[:, :, 1:-1, :]
    cond_yy = along_ydir[1]
    face_north = harmonic(cond_yy[:, :, 1:-1], cond_yy[:, :, 2:])
    face_south = harmonic(cond_yy[:, :, :-2], cond_yy[:, :, 1:-1])
    source_y = jnp.stack(
        [
            0.5 * (along_ydir[2][:, :, 2:] - along_ydir[2][:, :, :-2]),
            face_north - face_south,
            0.5 * (along_ydir[4][:, :, 2:] - along_ydir[4][:, :, :-2]),
        ]
    )
    return spike_solve(
        -face_south,
        damping + face_south + face_north,
        -face_north,
        damping * half_step + source_y,
        2,
        interface_y,
    )


def solution(mesh):
    in_specs = (P(None, None, "gx", "gy"), P(None, "gx", "gy"), P(), P())
    out_specs = P(None, None, "gx", "gy")
    return jax.shard_map(local, mesh=mesh, in_specs=in_specs, out_specs=out_specs, check_vma=False)
```

profile of v0, /device:TPU:0, one launch (start us, length us, event | category | flops | bytes accessed | tf_op | source)
XLA Modules:
  0.0 70.5 jit_solution(12789829236502406646)
XLA Ops:
  0.0 0.7 pad_maximum_fusion.15
  0.7 0.3 slice_reduce_fusion.9
  1.0 1.1 %compare_bitcast_fusion.7 = (pred[256,128]{1,0:T(8,128)(4,1)S(1)}, pred[256,128]{1,0:T(8,128)(4,1)S(1)}, pred[256,128]{1,0:T(8,128)(4,1)S(1)}, pred[256,128]{1,0...) fusion(s32[1,256,128]{2,1,0:T(8,128)} %param.5), kind=kLoop, calls=%fused_computation.147 | loop fusion | flops 262144 | bytes 393216 | tf_op jit(solution)/shard_map/jit(_where)/broadcast_in_dim | solution.py:136
  3.1 0.3 select_select_fusion
  3.6 5.5 %collective-permute-start.1 = (f32[5,1,1,128]{2,3,1,0:T(8,128)S(1)}, f32[5,1,1,128]{2,3,1,0:T(8,128)S(1)}, u32[]{:S(2)}, u32[]{:S(2)}) collective-permute-start(f32[5,1,1,128]{2,3,1,0:T(8,128)S(1)} %get-tuple-element.150), channel_id=1, source_target_pairs={{2,0},{4,2},{6,4},{8,6},{10,8},{12,10},{14,12},{16,14},{18,16},{20... | collective-permute-start | bytes 7688 | tf_op jit(solution)/shard_map/ppermute | solution.py:21
  9.0 0.6 iota_compare_fusion.5
  9.6 0.6 fusion.77
  10.2 0.5 iota_compare_fusion.4
  10.7 0.5 iota_compare_fusion.3
  11.2 0.6 fusion.76
  12.1 1.6 %collective-permute-done.1 = f32[5,1,1,128]{2,3,1,0:T(8,128)S(1)} collective-permute-done((f32[5,1,1,128]{2,3,1,0:T(8,128)S(1)}, f32[5,1,1,128]{2,3,1,0:T(8,128)S(1)}, u32[]{:S(2)}, u32[]{:S(2)}) %collective-permute-start.1) | collective-permute-done | bytes 2592 | tf_op jit(solution)/shard_map/ppermute | solution.py:21
  13.6 4.6 %collective-permute-done = f32[5,1,1,128]{2,3,1,0:T(8,128)S(1)} collective-permute-done((f32[5,1,1,128]{2,3,1,0:T(8,128)S(1)}, f32[5,1,1,128]{2,3,1,0:T(8,128)S(1)}, u32[]{:S(2)}, u32[]{:S(2)}) %collective-permute-start) | collective-permute-done | bytes 2592 | tf_op jit(solution)/shard_map/ppermute | solution.py:19
  18.7 0.7 broadcast_select_fusion.3
  20.1 0.3 multiply_add_fusion.12
  21.4 0.3 multiply_add_fusion.11
  22.6 0.3 multiply_add_fusion.10
  28.8 0.7 %pad_maximum_fusion.13 = (f32[5,1,258,1]{2,3,1,0:T(1,128)}, f32[5,1,258,1]{2,3,1,0:T(1,128)}) fusion(f32[5,1,1,128]{2,3,1,0:T(8,128)S(1)} %collective-permute-done.1, f32[5,1,256,128]{2,3,1,0:T(8,128)S(1)} %select_select_fusion, f32[5,1,1,128]{2,3,1,0:T(8,128)S(1)} %collective-permute-done), kind=kLoop, calls=%fused_computation.248 | loop fusion | flops 5160 | bytes 670800 | tf_op jit(solution)/shard_map/slice | solution.py:16
  29.6 1.6 %collective-permute-start.3 = (f32[5,1,258,1]{2,3,1,0:T(1,128)}, f32[5,1,258,1]{2,3,1,0:T(1,128)S(1)}, u32[]{:S(2)}, u32[]{:S(2)}) collective-permute-start(f32[5,1,258,1]{2,3,1,0:T(1,128)} %get-tuple-element.112), channel_id=1, source_target_pairs={{1,0},{0,1},{3,2},{2,3},{5,4},{4,5},{7,6},{6,7},{9,8},{8,9},{11,10... | collective-permute-start | bytes 15488 | tf_op jit(solution)/shard_map/ppermute | solution.py:21
  31.2 0.5 collective-permute-start.2
  31.8 0.6 copy.142
  32.5 0.8 %collective-permute-done.4 = f32[5,1,1,128]{2,3,1,0:T(8,128)S(1)} collective-permute-done((f32[5,1,1,128]{2,3,1,0:T(8,128)S(1)}, f32[5,1,1,128]{2,3,1,0:T(8,128)S(1)}, u32[]{:S(2)}, u32[]{:S(2)}) %collective-permute-start.4) | collective-permute-done | bytes 2592 | tf_op jit(solution)/shard_map/ppermute | solution.py:9
  33.5 0.8 %copy-done.1 = f32[1,256,128]{1,2,0:T(8,128)S(1)} copy-done((f32[1,256,128]{1,2,0:T(8,128)S(1)}, f32[1,256,128]{1,2,0:T(8,128)}, u32[]{:S(2)}) %copy-start.1) | copy-done | bytes 131096
  34.3 0.3 fusion.24
  34.6 0.6 copy-done.2
  35.2 18.7 %all_gather.6 = f32[6,1,16,128]{3,1,0,2:T(1,128)S(1)} all-gather(f32[6,1,1,128]{3,1,0,2:T(1,128)S(1)} %maximum_bitcast_fusion.5), channel_id=1, replica_groups=mesh['gx'=16,'gy'=2] {'gx'}, dimensions={2}, use_global_device_ids=true | all-gather | bytes 52224 | tf_op jit(solution)/shard_map/all_gather | solution.py:119
  55.2 0.7 copy-done.3
  56.0 0.6 copy-done.9
  56.8 0.7 copy-done.5
  61.2 1.6 %collective-permute-start.5 = (f32[5,1,256,1]{2,3,1,0:T(1,128)S(1)}, f32[5,1,256,1]{2,3,1,0:T(1,128)S(1)}, u32[]{:S(2)}, u32[]{:S(2)}) collective-permute-start(f32[5,1,256,1]{2,3,1,0:T(1,128)S(1)} %slice.1303), channel_id=1, source_target_pairs={{0,1},{1,0},{2,3},{3,2},{4,5},{5,4},{6,7},{7,6},{8,9},{9,8},{10,11... | collective-permute-start | bytes 15368 | tf_op jit(solution)/shard_map/ppermute | solution.py:9
  62.8 2.1 %collective-permute-done.5 = f32[5,1,256,1]{2,3,1,0:T(1,128)S(1)} collective-permute-done((f32[5,1,256,1]{2,3,1,0:T(1,128)S(1)}, f32[5,1,256,1]{2,3,1,0:T(1,128)S(1)}, u32[]{:S(2)}, u32[]{:S(2)}) %collective-permute-start.5) | collective-permute-done | bytes 5152 | tf_op jit(solution)/shard_map/ppermute | solution.py:9
  65.0 4.4 %all_gather.7 = f32[6,1,256,2]{2,1,0,3:T(1,128)S(1)} all-gather(f32[6,1,256,1]{2,1,0,3:T(1,128)S(1)} %maximum_bitcast_fusion.4), channel_id=1, replica_groups=mesh['gx'=16,'gy'=2] {'gy'}, dimensions={3}, use_global_device_ids=true | all-gather | bytes 18432 | tf_op jit(solution)/shard_map/all_gather | solution.py:128
  69.6 0.9 %copy.153 = f32[3,1,256,128]{3,2,1,0:T(8,128)} copy(f32[3,1,256,128]{2,3,1,0:T(8,128)S(1)} %fusion.1) | data formatting | bytes 786432 | tf_op jit(solution)/shard_map/jit(_where)/select_n | solution.py:105
  (229 shorter events, 15.1 us)
Async XLA Ops:
  3.4 8.5 %copy-start = (f32[3,1,256,128]{3,2,1,0:T(8,128)S(1)}, f32[3,1,256,128]{3,2,1,0:T(8,128)}, u32[]{:S(2)}) copy-start(f32[3,1,256,128]{3,2,1,0:T(8,128)} %param.4) | copy-start | bytes 1179652
  3.6 10.1 %collective-permute-start.1 = (f32[5,1,1,128]{2,3,1,0:T(8,128)S(1)}, f32[5,1,1,128]{2,3,1,0:T(8,128)S(1)}, u32[]{:S(2)}, u32[]{:S(2)}) collective-permute-start(f32[5,1,1,128]{2,3,1,0:T(8,128)S(1)} %get-tuple-element.150), channel_id=1, source_target_pairs={{2,0},{4,2},{6,4},{8,6},{10,8},{12,10},{14,12},{16,14},{18,16},{20... | collective-permute-start | bytes 7688 | tf_op jit(solution)/shard_map/ppermute | solution.py:21
  9.0 9.2 %collective-permute-start = (f32[5,1,1,128]{2,3,1,0:T(8,128)S(1)}, f32[5,1,1,128]{2,3,1,0:T(8,128)S(1)}, u32[]{:S(2)}, u32[]{:S(2)}) collective-permute-start(f32[5,1,1,128]{2,3,1,0:T(8,128)S(1)} %get-tuple-element.149), channel_id=1, source_target_pairs={{0,2},{2,4},{4,6},{6,8},{8,10},{10,12},{12,14},{14,16},{16,18},{18... | collective-permute-start | bytes 7688 | tf_op jit(solution)/shard_map/ppermute | solution.py:19
  11.8 7.9 %copy-start.4 = (pred[256]{0:T(512)(128)(4,1)}, pred[256]{0:T(512)(128)(4,1)S(1)}, u32[]{:S(2)}) copy-start(pred[256]{0:T(512)(128)(4,1)S(1)} %iota_compare_fusion.2) | copy-start | bytes 772
  28.6 4.8 %collective-permute-start.4 = (f32[5,1,1,128]{2,3,1,0:T(8,128)S(1)}, f32[5,1,1,128]{2,3,1,0:T(8,128)S(1)}, u32[]{:S(2)}, u32[]{:S(2)}) collective-permute-start(f32[5,1,1,128]{2,3,1,0:T(8,128)S(1)} %slice.1169), channel_id=1, source_target_pairs={{0,30},{2,0},{4,2},{6,4},{8,6},{10,8},{12,10},{14,12},{16,14},{18,... | collective-permute-start | bytes 7688 | tf_op jit(solution)/shard_map/ppermute | solution.py:9
  29.6 25.3 %collective-permute-start.3 = (f32[5,1,258,1]{2,3,1,0:T(1,128)}, f32[5,1,258,1]{2,3,1,0:T(1,128)S(1)}, u32[]{:S(2)}, u32[]{:S(2)}) collective-permute-start(f32[5,1,258,1]{2,3,1,0:T(1,128)} %get-tuple-element.112), channel_id=1, source_target_pairs={{1,0},{0,1},{3,2},{2,3},{5,4},{4,5},{7,6},{6,7},{9,8},{8,9},{11,10... | collective-permute-start | bytes 15488 | tf_op jit(solution)/shard_map/ppermute | solution.py:21
  31.2 23.7 %collective-permute-start.2 = (f32[5,1,258,1]{2,3,1,0:T(1,128)}, f32[5,1,258,1]{2,3,1,0:T(1,128)S(1)}, u32[]{:S(2)}, u32[]{:S(2)}) collective-permute-start(f32[5,1,258,1]{2,3,1,0:T(1,128)} %get-tuple-element.111), channel_id=1, source_target_pairs={{0,1},{1,0},{2,3},{3,2},{4,5},{5,4},{6,7},{7,6},{8,9},{9,8},{10,11... | collective-permute-start | bytes 15488 | tf_op jit(solution)/shard_map/ppermute | solution.py:19
  33.4 0.9 %copy-start.1 = (f32[1,256,128]{1,2,0:T(8,128)S(1)}, f32[1,256,128]{1,2,0:T(8,128)}, u32[]{:S(2)}) copy-start(f32[1,256,128]{1,2,0:T(8,128)} %get-tuple-element.102) | copy-start | bytes 393220
  34.6 0.6 copy-start.2
  55.2 0.7 copy-start.3
  55.9 0.7 copy-start.9
  56.0 0.7 copy-start.6
  56.0 0.7 copy-start.7
  56.0 0.6 copy-start.8
  56.8 0.7 copy-start.5
  61.2 3.7 %collective-permute-start.5 = (f32[5,1,256,1]{2,3,1,0:T(1,128)S(1)}, f32[5,1,256,1]{2,3,1,0:T(1,128)S(1)}, u32[]{:S(2)}, u32[]{:S(2)}) collective-permute-start(f32[5,1,256,1]{2,3,1,0:T(1,128)S(1)} %slice.1303), channel_id=1, source_target_pairs={{0,1},{1,0},{2,3},{3,2},{4,5},{5,4},{6,7},{7,6},{8,9},{9,8},{10,11... | collective-permute-start | bytes 15368 | tf_op jit(solution)/shard_map/ppermute | solution.py:9
where the time goes:
time: 70.8 us; the launch traced here: 70.5 us
  blocking collectives  23.1 us (33%)
  other arithmetic  15.5 us (22%)
  local copies, waits for them, and re-layouts  12 us (17%)
  starting transfers between devices  9.31 us (13%)
  waiting for transfers between devices  9.1 us (13%)
  between operations  1.55 us (2%)
    all_gather x1, blocking collectives, interface_x(): gathered = lax.all_gather(rows_here, 'gx', axis=2, tiled=True)  18.7 us
    ppermute x2, starting transfers between devices, padded_2(): lax.ppermute(head, axis, [((i + 1) % count, i) for i in range(count)])  7.05 us
    ppermute x2, waiting for transfers between devices, padded_2(): lax.ppermute(tail, axis, [(i, (i + 1) % count) for i in range(count)])  4.61 us
    all_gather x1, blocking collectives, interface_y(): gathered = lax.all_gather(rows_here, 'gy', axis=3, tiled=True)  4.36 us
    slice x47, local copies, waits for them, and re-layouts, neighbour(): retained = lax.slice_in_dim(values, 0, extent - offset, axis=axis_dim)  3.91 us
    unnamed x28, local copies, waits for them, and re-layouts  3.57 us
    add x16, other arithmetic, cyclic_reduce(): forcing + factor_low[None] * rest_before + factor_high[None] * rest_after  3.03 us
    ppermute x2, waiting for transfers between devices, shifted_2(): lax.ppermute(shard, axis, [(i, (i + by) % size) for i in range(size)])  2.92 us
  transfers between devices with their start and end apart: 6, of which 4 were waited for; matrix products, arithmetic and copies ran while one was open for 8% of the time, Pallas kernels for 0%

commit v1 on v0

--- a/solution.py
+++ b/solution.py
@@ -1,7 +1,37 @@
+import functools
 import jax
 import jax.numpy as jnp
 from jax import lax
 from jax.sharding import PartitionSpec as P
+
+
+def supply_cubes(matrix, dim_k):
+    piece_now = list(matrix.shape[1:])
+    piece_now[dim_k] *= matrix.shape[0]
+    taken_in = jnp.moveaxis(matrix, 0, dim_k).reshape(piece_now)
+    return taken_in
+
+
+def remake_the_lines(chunk, row_axis):
+    last = chunk[None]
+    n_shards = lax.axis_size(row_axis)
+    for nth in range(n_shards.bit_length() - 1):
+        before = 1 << nth
+        high = lax.ppermute(
+            last, row_axis, list(map(lambda j0: (j0, j0 ^ before), range(n_shards)))
+        )
+        tall = jnp.stack([last, high])
+        formed = lax.axis_index(row_axis) >> nth & 1
+        last = jnp.where(formed == 0, tall, tall[::-1]).reshape(-1, *chunk.shape)
+    return last
+
+
+def edit_sections(a0, vector, on_dim):
+    latest = supply_cubes(remake_the_lines(a0, vector), on_dim)
+    return latest
+
+
+recover_the_tracks = functools.partial(edit_sections, vector="gx", on_dim=2)
 
 
 def shifted_2(shard, axis, by):
@@ -116,7 +146,7 @@
     my_index = lax.axis_index("gx")
     next_head = shifted_2(head_row, "gx", -1)
     rows_here = reduced_rows(tail_row, next_head, low_last, main_last, high_last, force_last)
-    gathered = lax.all_gather(rows_here, "gx", axis=2, tiled=True)
+    gathered = recover_the_tracks(rows_here)
     solution = cyclic_reduce(gathered[0], gathered[1], gathered[2], gathered[3:], 1, True)
     return pick_values(solution, members, my_index, 2)
 

time: 70.8 us -> 65.1 us (0.919)
  blocking collectives: 23.1 us -> 4.36 us
  waiting for transfers between devices: 9.1 us -> 18.7 us
  starting transfers between devices: 9.31 us -> 11.9 us
    all_gather x1 -> x0, blocking collectives: 18.7 us -> none  [interface_x(): gathered = lax.all_gather(rows_here, 'gx', axis=2, tiled=True)]
    ppermute x0 -> x4, waiting for transfers between devices: none -> 9.73 us  [remake_the_lines(): lax.ppermute(last, row_axis, list(map(lambda j0: (j0, j0 ^ before), range...]
    ppermute x0 -> x4, starting transfers between devices: none -> 2.45 us  [remake_the_lines(): lax.ppermute(last, row_axis, list(map(lambda j0: (j0, j0 ^ before), range...]
    unnamed x28, local copies, waits for them, and re-layouts: 3.57 us -> 4.29 us
    add x13 -> x16, other arithmetic: 1.4 us -> 1.49 us  [cyclic_reduce(): main_diag = main_diag + factor_low * high_before + factor_high * low_after]
    mul x16 -> x15, other arithmetic: 1.79 us -> 1.75 us  [cyclic_reduce(): factor_low[None] * rest_before]
  transfers between devices with their start and end apart: 6 -> 10, of which waited for: 4 -> 7; matrix products, arithmetic and copies ran while one was open for 8% -> 11% of each run, Pallas kernels for 0% -> 0%
where the time goes in v1:
time: 65.1 us; the launch traced here: 64.9 us
  waiting for transfers between devices  18.7 us (29%)
  other arithmetic  15.5 us (24%)
  local copies, waits for them, and re-layouts  12.7 us (20%)
  starting transfers between devices  11.9 us (18%)
  blocking collectives  4.36 us (7%)
  between operations  1.63 us (3%)
    ppermute x4, waiting for transfers between devices, remake_the_lines(): lax.ppermute(last, row_axis, list(map(lambda j0: (j0, j0 ^ before), range...  9.73 us
    ppermute x2, starting transfers between devices, padded_2(): lax.ppermute(head, axis, [((i + 1) % count, i) for i in range(count)])  7.05 us
    ppermute x2, waiting for transfers between devices, padded_2(): lax.ppermute(tail, axis, [(i, (i + 1) % count) for i in range(count)])  4.61 us
    all_gather x1, blocking collectives, interface_y(): gathered = lax.all_gather(rows_here, 'gy', axis=3, tiled=True)  4.36 us
    unnamed x28, local copies, waits for them, and re-layouts  4.29 us
    slice x47, local copies, waits for them, and re-layouts, neighbour(): retained = lax.slice_in_dim(values, 0, extent - offset, axis=axis_dim)  3.91 us
    add x16, other arithmetic, cyclic_reduce(): forcing + factor_low[None] * rest_before + factor_high[None] * rest_after  2.89 us
    ppermute x2, waiting for transfers between devices, shifted_2(): lax.ppermute(shard, axis, [(i, (i + by) % size) for i in range(size)])  2.86 us
  transfers between devices with their start and end apart: 10, of which 7 were waited for; matrix products, arithmetic and copies ran while one was open for 11% of the time, Pallas kernels for 0%

profile of v1, /device:TPU:0, one launch (start us, length us, event | category | flops | bytes accessed | tf_op | source)
XLA Modules:
  0.0 64.9 jit_solution(12969397049228867971)
XLA Ops:
  0.0 0.7 %pad_maximum_fusion.19 = f32[5,8]{1,0:T(8,128)S(1)} fusion(f32[3,8]{1,0:T(4,128)} %param.7, f32[2,8]{1,0:T(2,128)} %param.6), kind=kLoop, calls=%fused_computation.276 | loop fusion | flops 40 | bytes 320 | tf_op jit(solution)/shard_map/concatenate | solution.py:175
  1.0 1.1 %compare_bitcast_fusion.7 = (pred[256,128]{1,0:T(8,128)(4,1)S(1)}, pred[256,128]{1,0:T(8,128)(4,1)S(1)}, pred[256,128]{1,0:T(8,128)(4,1)S(1)}, pred[256,128]{1,0...) fusion(s32[1,256,128]{2,1,0:T(8,128)} %param.5), kind=kLoop, calls=%fused_computation.147 | loop fusion | flops 262144 | bytes 393216 | tf_op jit(solution)/shard_map/jit(_where)/broadcast_in_dim | solution.py:166
  3.1 0.3 select_select_fusion
  3.6 5.5 %collective-permute-start.1 = (f32[5,1,1,128]{2,3,1,0:T(8,128)S(1)}, f32[5,1,1,128]{2,3,1,0:T(8,128)S(1)}, u32[]{:S(2)}, u32[]{:S(2)}) collective-permute-start(f32[5,1,1,128]{2,3,1,0:T(8,128)S(1)} %get-tuple-element.151), channel_id=1, source_target_pairs={{2,0},{4,2},{6,4},{8,6},{10,8},{12,10},{14,12},{16,14},{18,16},{20... | collective-permute-start | bytes 7688 | tf_op jit(solution)/shard_map/ppermute | solution.py:51
  9.0 0.6 iota_compare_fusion.5
  9.6 0.6 fusion.77
  10.2 0.6 iota_compare_fusion.3
  10.8 0.6 fusion.78
  11.4 0.5 iota_compare_fusion.4
  12.1 1.5 %collective-permute-done.1 = f32[5,1,1,128]{2,3,1,0:T(8,128)S(1)} collective-permute-done((f32[5,1,1,128]{2,3,1,0:T(8,128)S(1)}, f32[5,1,1,128]{2,3,1,0:T(8,128)S(1)}, u32[]{:S(2)}, u32[]{:S(2)}) %collective-permute-start.1) | collective-permute-done | bytes 2592 | tf_op jit(solution)/shard_map/ppermute | solution.py:51
  13.6 4.6 %collective-permute-done = f32[5,1,1,128]{2,3,1,0:T(8,128)S(1)} collective-permute-done((f32[5,1,1,128]{2,3,1,0:T(8,128)S(1)}, f32[5,1,1,128]{2,3,1,0:T(8,128)S(1)}, u32[]{:S(2)}, u32[]{:S(2)}) %collective-permute-start) | collective-permute-done | bytes 2592 | tf_op jit(solution)/shard_map/ppermute | solution.py:49
  18.7 0.7 %broadcast_select_fusion.3 = (f32[1,256,128]{1,2,0:T(8,128)S(1)}, f32[1,256,128]{1,2,0:T(8,128)}, f32[1,1,256,128]{2,3,1,0:T(8,128)S(1)}) fusion(pred[256]{0:T(512)(128)(4,1)S(1)} %iota_compare_fusion.2, f32[1,256,128]{1,2,0:T(8,128)S(1)} %get-tuple-element.155, f32[1,256,128]{1,2,0:T(8,128)S(1)} %get-tuple-element.69), kind=kLoop, calls=%fused_computation.163 | loop fusion | flops 131072 | bytes 655616 | tf_op jit(solution)/shard_map/jit(_where)/select_n | solution.py:118
  28.6 0.3 collective-permute-start.4
  29.0 0.7 %pad_maximum_fusion.16 = (f32[5,1,258,1]{2,3,1,0:T(1,128)}, f32[5,1,258,1]{2,3,1,0:T(1,128)}) fusion(f32[5,1,1,128]{2,3,1,0:T(8,128)S(1)} %collective-permute-done.1, f32[5,1,256,128]{2,3,1,0:T(8,128)S(1)} %select_select_fusion, f32[5,1,1,128]{2,3,1,0:T(8,128)S(1)} %collective-permute-done), kind=kLoop, calls=%fused_computation.259 | loop fusion | flops 5160 | bytes 670800 | tf_op jit(solution)/shard_map/slice | solution.py:46
  29.8 1.6 %collective-permute-start.3 = (f32[5,1,258,1]{2,3,1,0:T(1,128)}, f32[5,1,258,1]{2,3,1,0:T(1,128)S(1)}, u32[]{:S(2)}, u32[]{:S(2)}) collective-permute-start(f32[5,1,258,1]{2,3,1,0:T(1,128)} %get-tuple-element.113), channel_id=1, source_target_pairs={{1,0},{0,1},{3,2},{2,3},{5,4},{4,5},{7,6},{6,7},{9,8},{8,9},{11,10... | collective-permute-start | bytes 15488 | tf_op jit(solution)/shard_map/ppermute | solution.py:51
  31.4 0.5 collective-permute-start.2
  32.0 0.7 %copy.137 = f32[3,1,1,128]{3,2,1,0:T(1,128)} copy(f32[3,1,1,128]{2,3,1,0:T(8,128)S(1)} %slice.1175) | data formatting | bytes 3072 | tf_op jit(solution)/shard_map/slice | solution.py:130
  32.8 0.8 %collective-permute-done.4 = f32[5,1,1,128]{2,3,1,0:T(8,128)S(1)} collective-permute-done((f32[5,1,1,128]{2,3,1,0:T(8,128)S(1)}, f32[5,1,1,128]{2,3,1,0:T(8,128)S(1)}, u32[]{:S(2)}, u32[]{:S(2)}) %collective-permute-start.4) | collective-permute-done | bytes 2592 | tf_op jit(solution)/shard_map/ppermute | solution.py:39
  33.7 0.8 %copy-done.1 = f32[1,256,128]{1,2,0:T(8,128)S(1)} copy-done((f32[1,256,128]{1,2,0:T(8,128)S(1)}, f32[1,256,128]{1,2,0:T(8,128)}, u32[]{:S(2)}) %copy-start.1) | copy-done | bytes 131096
  34.8 0.7 %copy-done.2 = f32[3,1,1,128]{3,2,1,0:T(1,128)S(1)} copy-done((f32[3,1,1,128]{3,2,1,0:T(1,128)S(1)}, f32[3,1,1,128]{3,2,1,0:T(1,128)}, u32[]{:S(2)}) %copy-start.2) | copy-done | bytes 1560
  35.8 0.6 copy-done.3
  36.6 0.6 copy-done.8
  37.4 0.6 copy-done.6
  39.9 3.6 %collective-permute-done.6 = f32[2,6,1,1,128]{4,2,3,1,0:T(1,128)S(1)} collective-permute-done((f32[2,6,1,1,128]{4,2,3,1,0:T(1,128)S(1)}, f32[2,6,1,1,128]{4,2,3,1,0:T(1,128)S(1)}, u32[]{:S(2)}, u32[]{:S(2)}) %collective-permute-start.6) | collective-permute-done | bytes 6176 | tf_op jit(solution)/shard_map/ppermute | solution.py:20
  43.8 3.5 %collective-permute-done.7 = f32[4,6,1,1,128]{4,2,3,1,0:T(1,128)S(1)} collective-permute-done((f32[4,6,1,1,128]{4,2,3,1,0:T(1,128)S(1)}, f32[4,6,1,1,128]{4,2,3,1,0:T(1,128)S(1)}, u32[]{:S(2)}, u32[]{:S(2)}) %collective-permute-start.7) | collective-permute-done | bytes 12320 | tf_op jit(solution)/shard_map/ppermute | solution.py:20
  47.4 2.1 %collective-permute-start.8 = (f32[8,6,1,1,128]{4,0,1,3,2:T(8,128)S(1)}, f32[8,6,1,1,128]{4,0,1,3,2:T(8,128)S(1)}, u32[]{:S(2)}, u32[]{:S(2)}) collective-permute-start(f32[8,6,1,1,128]{4,0,1,3,2:T(8,128)S(1)} %copy.141), channel_id=1, source_target_pairs={{0,16},{2,18},{4,20},{6,22},{8,24},{10,26},{12,28},{14,30},{16,0},... | collective-permute-start | bytes 73736 | tf_op jit(solution)/shard_map/ppermute | solution.py:20
  49.5 2.6 %collective-permute-done.8 = f32[8,6,1,1,128]{4,0,1,3,2:T(8,128)S(1)} collective-permute-done((f32[8,6,1,1,128]{4,0,1,3,2:T(8,128)S(1)}, f32[8,6,1,1,128]{4,0,1,3,2:T(8,128)S(1)}, u32[]{:S(2)}, u32[]{:S(2)}) %collective-permute-start.8) | collective-permute-done | bytes 24608 | tf_op jit(solution)/shard_map/ppermute | solution.py:20
  52.9 0.7 %copy-done.5 = pred[256]{0:T(512)(128)(4,1)S(1)} copy-done((pred[256]{0:T(512)(128)(4,1)S(1)}, pred[256]{0:T(512)(128)(4,1)}, u32[]{:S(2)}) %copy-start.5) | copy-done | bytes 280
  55.6 1.6 %collective-permute-start.9 = (f32[5,1,256,1]{2,3,1,0:T(1,128)S(1)}, f32[5,1,256,1]{2,3,1,0:T(1,128)S(1)}, u32[]{:S(2)}, u32[]{:S(2)}) collective-permute-start(f32[5,1,256,1]{2,3,1,0:T(1,128)S(1)} %slice.1306), channel_id=1, source_target_pairs={{0,1},{1,0},{2,3},{3,2},{4,5},{5,4},{6,7},{7,6},{8,9},{9,8},{10,11... | collective-permute-start | bytes 15368 | tf_op jit(solution)/shard_map/ppermute | solution.py:39
  57.2 2.1 %collective-permute-done.9 = f32[5,1,256,1]{2,3,1,0:T(1,128)S(1)} collective-permute-done((f32[5,1,256,1]{2,3,1,0:T(1,128)S(1)}, f32[5,1,256,1]{2,3,1,0:T(1,128)S(1)}, u32[]{:S(2)}, u32[]{:S(2)}) %collective-permute-start.9) | collective-permute-done | bytes 5152 | tf_op jit(solution)/shard_map/ppermute | solution.py:39
  59.3 4.4 %all_gather.3 = f32[6,1,256,2]{2,1,0,3:T(1,128)S(1)} all-gather(f32[6,1,256,1]{2,1,0,3:T(1,128)S(1)} %maximum_bitcast_fusion.4), channel_id=1, replica_groups=mesh['gx'=16,'gy'=2] {'gy'}, dimensions={3}, use_global_device_ids=true | all-gather | bytes 18432 | tf_op jit(solution)/shard_map/all_gather | solution.py:158
  63.9 0.9 %copy.147 = f32[3,1,256,128]{3,2,1,0:T(8,128)} copy(f32[3,1,256,128]{2,3,1,0:T(8,128)S(1)} %fusion.1) | data formatting | bytes 786432 | tf_op jit(solution)/shard_map/jit(_where)/select_n | solution.py:135
  (247 shorter events, 16.6 us)
Async XLA Ops:
  3.4 8.5 %copy-start = (f32[3,1,256,128]{3,2,1,0:T(8,128)S(1)}, f32[3,1,256,128]{3,2,1,0:T(8,128)}, u32[]{:S(2)}) copy-start(f32[3,1,256,128]{3,2,1,0:T(8,128)} %param.4) | copy-start | bytes 1179652
  3.6 10.1 %collective-permute-start.1 = (f32[5,1,1,128]{2,3,1,0:T(8,128)S(1)}, f32[5,1,1,128]{2,3,1,0:T(8,128)S(1)}, u32[]{:S(2)}, u32[]{:S(2)}) collective-permute-start(f32[5,1,1,128]{2,3,1,0:T(8,128)S(1)} %get-tuple-element.151), channel_id=1, source_target_pairs={{2,0},{4,2},{6,4},{8,6},{10,8},{12,10},{14,12},{16,14},{18,16},{20... | collective-permute-start | bytes 7688 | tf_op jit(solution)/shard_map/ppermute | solution.py:51
  9.0 9.2 %collective-permute-start = (f32[5,1,1,128]{2,3,1,0:T(8,128)S(1)}, f32[5,1,1,128]{2,3,1,0:T(8,128)S(1)}, u32[]{:S(2)}, u32[]{:S(2)}) collective-permute-start(f32[5,1,1,128]{2,3,1,0:T(8,128)S(1)} %get-tuple-element.150), channel_id=1, source_target_pairs={{0,2},{2,4},{4,6},{6,8},{8,10},{10,12},{12,14},{14,16},{16,18},{18... | collective-permute-start | bytes 7688 | tf_op jit(solution)/shard_map/ppermute | solution.py:49
  11.8 7.9 %copy-start.4 = (pred[256]{0:T(512)(128)(4,1)}, pred[256]{0:T(512)(128)(4,1)S(1)}, u32[]{:S(2)}) copy-start(pred[256]{0:T(512)(128)(4,1)S(1)} %iota_compare_fusion.2) | copy-start | bytes 772
  28.6 4.9 %collective-permute-start.4 = (f32[5,1,1,128]{2,3,1,0:T(8,128)S(1)}, f32[5,1,1,128]{2,3,1,0:T(8,128)S(1)}, u32[]{:S(2)}, u32[]{:S(2)}) collective-permute-start(f32[5,1,1,128]{2,3,1,0:T(8,128)S(1)} %slice.1172), channel_id=1, source_target_pairs={{0,30},{2,0},{4,2},{6,4},{8,6},{10,8},{12,10},{14,12},{16,14},{18,... | collective-permute-start | bytes 7688 | tf_op jit(solution)/shard_map/ppermute | solution.py:39
  29.8 5.8 %collective-permute-start.3 = (f32[5,1,258,1]{2,3,1,0:T(1,128)}, f32[5,1,258,1]{2,3,1,0:T(1,128)S(1)}, u32[]{:S(2)}, u32[]{:S(2)}) collective-permute-start(f32[5,1,258,1]{2,3,1,0:T(1,128)} %get-tuple-element.113), channel_id=1, source_target_pairs={{1,0},{0,1},{3,2},{2,3},{5,4},{4,5},{7,6},{6,7},{9,8},{8,9},{11,10... | collective-permute-start | bytes 15488 | tf_op jit(solution)/shard_map/ppermute | solution.py:51
  31.4 4.2 %collective-permute-start.2 = (f32[5,1,258,1]{2,3,1,0:T(1,128)}, f32[5,1,258,1]{2,3,1,0:T(1,128)S(1)}, u32[]{:S(2)}, u32[]{:S(2)}) collective-permute-start(f32[5,1,258,1]{2,3,1,0:T(1,128)} %get-tuple-element.112), channel_id=1, source_target_pairs={{0,1},{1,0},{2,3},{3,2},{4,5},{5,4},{6,7},{7,6},{8,9},{9,8},{10,11... | collective-permute-start | bytes 15488 | tf_op jit(solution)/shard_map/ppermute | solution.py:49
  33.6 0.9 %copy-start.1 = (f32[1,256,128]{1,2,0:T(8,128)S(1)}, f32[1,256,128]{1,2,0:T(8,128)}, u32[]{:S(2)}) copy-start(f32[1,256,128]{1,2,0:T(8,128)} %get-tuple-element.103) | copy-start | bytes 393220
  34.8 0.7 %copy-start.2 = (f32[3,1,1,128]{3,2,1,0:T(1,128)S(1)}, f32[3,1,1,128]{3,2,1,0:T(1,128)}, u32[]{:S(2)}) copy-start(f32[3,1,1,128]{3,2,1,0:T(1,128)} %copy.137) | copy-start | bytes 4612
  35.5 4.3 %collective-permute-start.5 = (f32[1,6,1,1,128]{4,0,3,2,1:T(1,128)S(1)}, f32[1,6,1,1,128]{4,0,3,2,1:T(1,128)S(1)}, u32[]{:S(2)}, u32[]{:S(2)}) collective-permute-start(f32[1,6,1,1,128]{4,0,3,2,1:T(1,128)S(1)} %fusion.191), channel_id=1, source_target_pairs={{0,2},{2,0},{4,6},{6,4},{8,10},{10,8},{12,14},{14,12},{16,18},{18,... | collective-permute-start | bytes 9224 | tf_op jit(solution)/shard_map/ppermute | solution.py:20
  35.8 0.7 %copy-start.3 = (pred[128]{0:T(512)(128)(4,1)S(1)}, pred[128]{0:T(512)(128)(4,1)}, u32[]{:S(2)}) copy-start(pred[128]{0:T(512)(128)(4,1)} %iota_compare_fusion.5) | copy-start | bytes 388
  36.6 0.7 %copy-start.8 = (pred[128]{0:T(512)(128)(4,1)S(1)}, pred[128]{0:T(512)(128)(4,1)}, u32[]{:S(2)}) copy-start(pred[128]{0:T(512)(128)(4,1)} %fusion.78) | copy-start | bytes 388
  36.6 0.7 %copy-start.9 = (pred[128]{0:T(512)(128)(4,1)S(1)}, pred[128]{0:T(512)(128)(4,1)}, u32[]{:S(2)}) copy-start(pred[128]{0:T(512)(128)(4,1)} %iota_compare_fusion.4) | copy-start | bytes 388
  37.4 0.7 %copy-start.6 = (pred[128]{0:T(512)(128)(4,1)S(1)}, pred[128]{0:T(512)(128)(4,1)}, u32[]{:S(2)}) copy-start(pred[128]{0:T(512)(128)(4,1)} %fusion.77) | copy-start | bytes 388
  37.4 0.7 %copy-start.7 = (pred[128]{0:T(512)(128)(4,1)S(1)}, pred[128]{0:T(512)(128)(4,1)}, u32[]{:S(2)}) copy-start(pred[128]{0:T(512)(128)(4,1)} %iota_compare_fusion.3) | copy-start | bytes 388
  39.8 3.7 %collective-permute-start.6 = (f32[2,6,1,1,128]{4,2,3,1,0:T(1,128)S(1)}, f32[2,6,1,1,128]{4,2,3,1,0:T(1,128)S(1)}, u32[]{:S(2)}, u32[]{:S(2)}) collective-permute-start(f32[2,6,1,1,128]{4,2,3,1,0:T(1,128)S(1)} %get-tuple-element.376), channel_id=1, source_target_pairs={{0,4},{2,6},{4,0},{6,2},{8,12},{10,14},{12,8},{14,10},{16,20},{18,... | collective-permute-start | bytes 18440 | tf_op jit(solution)/shard_map/ppermute | solution.py:20
  43.5 3.8 %collective-permute-start.7 = (f32[4,6,1,1,128]{4,2,3,1,0:T(1,128)S(1)}, f32[4,6,1,1,128]{4,2,3,1,0:T(1,128)S(1)}, u32[]{:S(2)}, u32[]{:S(2)}) collective-permute-start(f32[4,6,1,1,128]{4,2,3,1,0:T(1,128)S(1)} %bitcast.368), channel_id=1, source_target_pairs={{0,8},{2,10},{4,12},{6,14},{8,0},{10,2},{12,4},{14,6},{16,24},{18,... | collective-permute-start | bytes 36872 | tf_op jit(solution)/shard_map/ppermute | solution.py:20
  47.4 4.8 %collective-permute-start.8 = (f32[8,6,1,1,128]{4,0,1,3,2:T(8,128)S(1)}, f32[8,6,1,1,128]{4,0,1,3,2:T(8,128)S(1)}, u32[]{:S(2)}, u32[]{:S(2)}) collective-permute-start(f32[8,6,1,1,128]{4,0,1,3,2:T(8,128)S(1)} %copy.141), channel_id=1, source_target_pairs={{0,16},{2,18},{4,20},{6,22},{8,24},{10,26},{12,28},{14,30},{16,0},... | collective-permute-start | bytes 73736 | tf_op jit(solution)/shard_map/ppermute | solution.py:20
  52.9 0.7 %copy-start.5 = (pred[256]{0:T(512)(128)(4,1)S(1)}, pred[256]{0:T(512)(128)(4,1)}, u32[]{:S(2)}) copy-start(pred[256]{0:T(512)(128)(4,1)} %copy-done.4) | copy-start | bytes 772
  55.6 3.7 %collective-permute-start.9 = (f32[5,1,256,1]{2,3,1,0:T(1,128)S(1)}, f32[5,1,256,1]{2,3,1,0:T(1,128)S(1)}, u32[]{:S(2)}, u32[]{:S(2)}) collective-permute-start(f32[5,1,256,1]{2,3,1,0:T(1,128)S(1)} %slice.1306), channel_id=1, source_target_pairs={{0,1},{1,0},{2,3},{3,2},{4,5},{5,4},{6,7},{7,6},{8,9},{9,8},{10,11... | collective-permute-start | bytes 15368 | tf_op jit(solution)/shard_map/ppermute | solution.py:39
